TPU v7x, 512 devices: a whole 4x4x16 slice. The times are simulated.
512 devices in a mesh: row: 16 (over z), space: 32 (over y, x, core).
Axes of the slice: x: 4, y: 4, z: 16, core: 2. Of those that a mesh axis runs over, the one named last changes fastest.
Arguments:
- features: bfloat16 [8192, 128], P(('row', 'space')), may hold values from -6 to 6
- positions: float32 [3, 8192], P(None, ('row', 'space')), may hold values from -0.5 to 78, as said below
- species: int32 [8192], P(('row', 'space')), may hold values from 0 to 3
- ghost_list: int32 [16, 1024, 32], P('row', 'space'), may hold values from 0 to 15
- edge_recv: int32 [262144], P(('row', 'space')), may hold values from 0 to 16, as said below
- edge_send: int32 [262144], P(('row', 'space')), may hold values from 0 to 1039
- edge_vec: float32 [3, 262144], P(None, ('row', 'space')), may hold values from -5.8 to 5.8, as said below
- w_msg: bfloat16 [128, 256], replicated, may hold values from -0.5 to 0.5
- w_rad1: float32 [8, 128], replicated, may hold values from -2 to 2
- w_rad2: bfloat16 [128, 256], replicated, may hold values from -0.5 to 0.5
- w_up: bfloat16 [256, 128], replicated, may hold values from -0.375 to 0.375
- w_out: float32 [128], replicated, may hold values from -0.5 to 0.5
- hardness: float32 [4], replicated, may hold values from 2 to 4
- width: float32 [4], replicated, may hold values from 0.8 to 1.6
- chi_shift: float32 [4], replicated, may hold values from -1 to 1
- field: float32 [1], replicated, may hold values from 0.01 to 0.03
Outputs:
- new_features: bfloat16 [8192, 128], P(('row', 'space'))
- charges: float32 [8192], P(('row', 'space'))
- forces: float32 [3, 8192], P(None, ('row', 'space'))
- virial: float32 [6, 8192], P(None, ('row', 'space'))
Inputs may be any that keep to these rules, and one draw needn't show every extreme that they name: `edge_recv`: in every domain the edges are ordered by receiver; the slots in use fill the first whole blocks of 128 rows, a quarter of the blocks or more, and the other slots hold 16; some domain uses all its slots. `positions`: every two atoms are 1.5 or more apart. `edge_vec`: each edge's length lies between 1.2 and 5.8.
All inputs are finite; a program needn't handle non-finite values.
Results may differ from a plain program's by a relative error of at most 0.0045.
Values may be sent and summed in bfloat16 or wider, within the bound.
A program may use at most 64 MiB of HBM per device.

v0:
```python
import math
import jax
import jax.numpy as jnp
from jax import lax
from jax.sharding import PartitionSpec as P

ITERS = 2
cutoff = 6.0
message_scale = 0.125
two_over_root_pi = 2.0 / math.sqrt(math.pi)
inverse_root_pi = 1.0 / math.sqrt(math.pi)
pair_limit = 262144


def lookup(species, table):
    result = jnp.zeros(species.shape, jnp.float32)
    for kind in range(table.shape[0]):
        result = result + jnp.where(species == kind, table[kind], 0.0)
    return result


def pair_block(target, target_labels, source, source_labels, source_charge, forces):
    delta = target[:3, :, None] - source[:3, None, :]
    squared = jnp.sum(delta * delta, axis=0)
    same = target_labels[:, None] == source_labels[None, :]
    squared = jnp.where(same, 1.0, squared)
    inverse = lax.rsqrt(squared)
    radius = squared * inverse
    spread = target[3][:, None] * target[3][:, None] + source[3][None, :] * source[3][None, :]
    scale = lax.rsqrt(2.0 * spread)
    scaled = radius * scale
    smear = lax.erf(scaled)
    if forces:
        slope = (
            two_over_root_pi * scale * jnp.exp(-scaled * scaled) * inverse
            - smear * inverse * inverse
        )
        weight = jnp.where(same, 0.0, source_charge[None, :] * slope * inverse)
        first = jnp.sum(weight[None] * delta, axis=2)
        pairs = ((0, 0), (1, 1), (2, 2), (0, 1), (0, 2), (1, 2))
        second = jnp.stack(
            [jnp.sum(weight * delta[left] * delta[right], axis=1) for left, right in pairs]
        )
        return jnp.concatenate([first, second], axis=0)
    kernel = jnp.where(same, 0.0, smear * inverse)
    return jnp.sum(kernel * source_charge[None, :], axis=1)


def pair_sums(target, target_labels, source, source_labels, source_charge, forces):
    count = target.shape[1]
    extent = source.shape[1]
    block = extent
    while block * count > pair_limit and block % 2 == 0:
        block = block // 2
    turns = extent // block
    source_blocks = source.reshape(4, turns, block).transpose(1, 0, 2)
    label_blocks = source_labels.reshape(turns, block)
    charge_blocks = source_charge.reshape(turns, block)
    start_value = jnp.zeros((9, count) if forces else (count,), jnp.float32)

    def accumulate(carry, item):
        return (carry + pair_block(target, target_labels, item[0], item[1], item[2], forces), None)

    total, _ = lax.scan(accumulate, start_value, (source_blocks, label_blocks, charge_blocks))
    return total


def edge_terms(receive, sender_rows, vectors, projected, w_rad1, w_rad2, atoms):
    length = jnp.sqrt(jnp.sum(vectors * vectors, axis=0))
    unit = vectors / length
    order = jnp.arange(1, w_rad1.shape[0] + 1, dtype=jnp.int32).astype(jnp.float32)[:, None]
    ratio = length / cutoff
    envelope = (1.0 - ratio * ratio) * (1.0 - ratio * ratio)
    basis = jnp.sin(order * math.pi * ratio) / ratio * envelope
    mixed = lax.dot_general(
        basis, w_rad1, (((0,), (0,)), ((), ())), precision=lax.Precision.HIGHEST
    )
    radial = jax.nn.silu(mixed).astype(jnp.bfloat16)
    filters = jnp.dot(radial, w_rad2, preferred_element_type=jnp.float32)
    picked = jnp.take(projected, sender_rows, axis=0).astype(jnp.float32) * filters
    chans = w_rad1.shape[1]
    scalar = picked[:, :chans]
    carried = picked[:, chans:]
    joined = [
        scalar,
        unit[0][:, None] * carried,
        unit[1][:, None] * carried,
        unit[2][:, None] * carried,
    ]
    message = jnp.concatenate(joined, axis=1).astype(jnp.bfloat16)
    onehot = (jnp.arange(atoms, dtype=jnp.int32)[:, None] == receive[None, :]).astype(jnp.bfloat16)
    return jnp.dot(onehot, message, preferred_element_type=jnp.float32)


def shards(
    features,
    positions,
    species,
    ghost_list,
    edge_recv,
    edge_send,
    edge_vec,
    w_msg,
    w_rad1,
    w_rad2,
    w_up,
    w_out,
    hardness,
    width,
    chi_shift,
    field,
):
    atoms = features.shape[0]
    chans = features.shape[1]
    lanes = lax.axis_size("space")
    row_at = lax.axis_index("row")
    space_at = lax.axis_index("space")
    lists = ghost_list[0]
    outgoing = jnp.take(features, lists.reshape(-1), axis=0).reshape(lanes, lists.shape[1], chans)
    ghost_rows = jnp.einsum(
        "dkc,cf->dkf",
        lax.all_to_all(outgoing, "space", split_axis=0, concat_axis=0, tiled=True),
        w_msg,
        preferred_element_type=jnp.float32,
    ).astype(jnp.bfloat16)
    own_rows = jnp.dot(features, w_msg, preferred_element_type=jnp.float32).astype(jnp.bfloat16)
    projected = jnp.concatenate([own_rows, ghost_rows.reshape(-1, 2 * chans)], axis=0)
    summed = edge_terms(edge_recv, edge_send, edge_vec, projected, w_rad1, w_rad2, atoms)
    summed = summed * message_scale
    vector_part = summed[:, chans:].reshape(atoms, 3, chans)
    invariant = jnp.concatenate(
        [summed[:, :chans], jnp.sum(vector_part * vector_part, axis=1)], axis=1
    ).astype(jnp.bfloat16)
    hidden = jax.nn.silu(jnp.dot(invariant, w_up, preferred_element_type=jnp.float32))
    new_features = (features.astype(jnp.float32) + hidden).astype(jnp.bfloat16)
    chi = jnp.dot(hidden, w_out, precision=lax.Precision.HIGHEST) + lookup(species, chi_shift)
    sigma = lookup(species, width)
    diag = lookup(species, hardness) + inverse_root_pi / sigma
    placed = jnp.concatenate([positions, sigma[None, :]], axis=0)
    own_labels = (row_at * lanes + space_at) * atoms + jnp.arange(atoms, dtype=jnp.int32)
    everyone = lax.all_gather(placed, ("row", "space"), axis=1, tiled=True)
    all_labels = jnp.arange(everyone.shape[1], dtype=jnp.int32)

    def spread_out(vector):
        return lax.all_gather(vector, ("row", "space"), axis=0, tiled=True)

    rhs = field[0] * positions[2] - chi
    charges = jnp.zeros_like(rhs)
    residual = rhs

    def squares(current):
        return lax.psum(jnp.sum(current * current), ("row", "space"))

    direction = residual
    norm_now = squares(residual)
    for step in range(ITERS):
        image = diag * direction + pair_sums(
            placed, own_labels, everyone, all_labels, spread_out(direction), False
        )
        alpha = norm_now / lax.psum(jnp.sum(direction * image), ("row", "space"))
        charges = charges + alpha * direction
        residual = residual - alpha * image
        fresh = squares(residual)
        direction = residual + fresh / norm_now * direction
        norm_now = fresh
    sums = pair_sums(placed, own_labels, everyone, all_labels, spread_out(charges), True)
    pull = -charges[None, :] * sums[:3]
    forces = jnp.concatenate([pull[:2], pull[2:] + (charges * field[0])[None, :]], axis=0)
    virial = 0.5 * charges[None, :] * sums[3:]
    return (new_features, charges, forces, virial)


def solution(mesh):
    return jax.shard_map(
        shards,
        mesh=mesh,
        in_specs=(
            P(("row", "space"), None),
            P(None, ("row", "space")),
            P(("row", "space")),
            P("row", "space", None),
            P(("row", "space")),
            P(("row", "space")),
            P(None, ("row", "space")),
            P(),
            P(),
            P(),
            P(),
            P(),
            P(),
            P(),
            P(),
            P(),
        ),
        out_specs=(
            P(("row", "space"), None),
            P(("row", "space")),
            P(None, ("row", "space")),
            P(None, ("row", "space")),
        ),
        check_vma=False,
    )
```

profile of v0, /device:TPU:1, one launch (start us, length us, event | category | flops | bytes accessed | tf_op | source)
XLA Modules:
  0.0 782.4 jit_solution(4420758810562936162)
XLA Ops:
  0.6 0.8 reshape_squeeze.6
  1.5 0.7 compare_and_fusion
  2.3 3.6 gather_fusion
  5.9 0.9 broadcast_select_fusion
  6.8 10.4 %all-to-all-start = ((bf16[32,32,128]{2,1,0:T(8,128)(2,1)}), bf16[32,32,128]{2,1,0:T(8,128)(2,1)S(1)}, u32[]{:S(2)}, u32[]{:S(2)}) async-start(bf16[32,32,128]{2,1,0:T(8,128)(2,1)} %broadcast_select_fusion), calls=%async_computation | async-start | bytes 524288 | tf_op jit(solution)/shard_map/all_to_all | solution.py:122
  18.0 0.7 fusion.42
  18.7 0.7 fusion.43
  19.3 0.6 fusion.44
  20.1 2.5 fusion.39
  22.7 138.5 %all-gather = f32[512,16,4]{1,2,0:T(4,128)S(1)} all-gather(f32[1,16,4]{1,2,0:T(4,128)S(1)} %maximum_bitcast_fusion), channel_id=1, replica_groups=mesh['row'=16,'space'=32] {'row','space'}, dimensions={0}, use_global_device_ids=true | all-gather | bytes 131328 | tf_op jit(solution)/shard_map/all_gather | solution.py:141
  161.2 0.6 reshape.216
  161.9 0.7 multiply_convert_fusion.3
  163.2 2.0 gather_fusion.1
  165.3 1.1 convolution_multiply_fusion
  166.9 0.4 copy-done.2
  167.3 0.7 add_convert_fusion
  168.0 2.6 fusion.1
  170.9 100.5 %all-reduce = f32[8192]{0:T(1024)S(1)} all-reduce(f32[8192]{0:T(1024)S(1)} %dynamic-update-slice), channel_id=1, replica_groups=mesh['row'=16,'space'=32] {'row','space'}, use_global_device_ids=true, to_apply=%add | all-reduce | flops 8192 | bytes 65536
  271.4 0.5 multiply_reduce_fusion.8
  271.9 3.2 multiply_reduce_fusion.12
  275.1 99.4 %all-reduce.3 = (f32[]{:T(128)}, f32[]{:T(128)}) all-reduce(f32[]{:T(128)} %get-tuple-element.67, f32[]{:T(128)} %get-tuple-element.66), channel_id=1, replica_groups=mesh['row'=16,'space'=32] {'row','space'}, use_global_device_ids=true, to_apply=%region_3.4 | all-reduce | flops 2 | bytes 16 | tf_op jit(solution)/shard_map/psum | solution.py:152
  375.8 0.6 multiply_reduce_fusion.11
  376.4 99.4 %psum.30 = f32[]{:T(128)} all-reduce(f32[]{:T(128)} %get-tuple-element.83), channel_id=1, replica_groups=mesh['row'=16,'space'=32] {'row','space'}, use_global_device_ids=true, to_apply=%region_9.10 | all-reduce | flops 1 | bytes 8 | tf_op jit(solution)/shard_map/psum | solution.py:152
  477.2 100.3 %all-reduce.1 = f32[8192]{0:T(1024)S(1)} all-reduce(f32[8192]{0:T(1024)S(1)} %get-tuple-element.81), channel_id=1, replica_groups=mesh['row'=16,'space'=32] {'row','space'}, use_global_device_ids=true, to_apply=%add.1 | all-reduce | flops 8192 | bytes 65536
  577.5 0.3 multiply_reduce_fusion.7
  577.9 0.6 multiply_reduce_fusion.10
  578.5 99.4 %psum.31 = f32[]{:T(128)} all-reduce(f32[]{:T(128)} %multiply_reduce_fusion.10), channel_id=1, replica_groups=mesh['row'=16,'space'=32] {'row','space'}, use_global_device_ids=true, to_apply=%region_12.13 | all-reduce | flops 1 | bytes 8 | tf_op jit(solution)/shard_map/psum | solution.py:160
  679.6 100.3 %all-reduce.2 = f32[8192]{0:T(1024)S(1)} all-reduce(f32[8192]{0:T(1024)S(1)} %dynamic-update-slice.2), channel_id=1, replica_groups=mesh['row'=16,'space'=32] {'row','space'}, use_global_device_ids=true, to_apply=%add.2 | all-reduce | flops 8192 | bytes 65536
  779.8 0.9 multiply_reduce_fusion.2
  780.8 0.4 multiply_reduce_fusion
  781.2 0.6 pad_maximum_fusion.1
  781.8 0.6 broadcast_multiply_fusion
  (68 shorter events, 2.3 us)
Async XLA Ops:
  0.6 19.3 %copy-start = (bf16[128,256]{1,0:T(8,128)(2,1)S(1)}, bf16[128,256]{1,0:T(8,128)(2,1)}, u32[]{:S(2)}) copy-start(bf16[128,256]{1,0:T(8,128)(2,1)} %param.23) | copy-start | bytes 196612
  2.2 15.0 %copy-start.5 = (s32[512]{0:T(512)S(1)}, s32[512]{0:T(512)}, u32[]{:S(2)}) copy-start(s32[512]{0:T(512)} %param.21) | copy-start | bytes 6148
  2.2 15.7 %copy-start.3 = (f32[3,512]{1,0:T(4,128)S(1)}, f32[3,512]{1,0:T(4,128)}, u32[]{:S(2)}) copy-start(f32[3,512]{1,0:T(4,128)} %param.22) | copy-start | bytes 18436
  2.2 15.8 %copy-start.6 = (f32[4]{0:T(128)S(1)}, f32[4]{0:T(128)}, u32[]{:S(2)}) copy-start(f32[4]{0:T(128)} %param.28) | copy-start | bytes 52
  2.3 16.4 %copy-start.7 = (f32[4]{0:T(128)S(1)}, f32[4]{0:T(128)}, u32[]{:S(2)}) copy-start(f32[4]{0:T(128)} %param.29) | copy-start | bytes 52
  2.3 17.1 %copy-start.8 = (f32[4]{0:T(128)S(1)}, f32[4]{0:T(128)}, u32[]{:S(2)}) copy-start(f32[4]{0:T(128)} %param.30) | copy-start | bytes 52
  2.3 17.7 %copy-start.1 = (bf16[16,128]{1,0:T(8,128)(2,1)S(1)}, bf16[16,128]{1,0:T(8,128)(2,1)}, u32[]{:S(2)}) copy-start(bf16[16,128]{1,0:T(8,128)(2,1)} %param.16) | copy-start | bytes 12292
  2.3 17.8 %copy-start.9 = (s32[16]{0:T(128)S(1)}, s32[16]{0:T(128)}, u32[]{:S(2)}) copy-start(s32[16]{0:T(128)} %param.18) | copy-start | bytes 196
  2.3 20.4 %copy-start.4 = (f32[3,16]{1,0:T(4,128)S(1)}, f32[3,16]{1,0:T(4,128)}, u32[]{:S(2)}) copy-start(f32[3,16]{1,0:T(4,128)} %param.17) | copy-start | bytes 580
  6.8 156.0 %all-to-all-start = ((bf16[32,32,128]{2,1,0:T(8,128)(2,1)}), bf16[32,32,128]{2,1,0:T(8,128)(2,1)S(1)}, u32[]{:S(2)}, u32[]{:S(2)}) async-start(bf16[32,32,128]{2,1,0:T(8,128)(2,1)} %broadcast_select_fusion), calls=%async_computation | async-start | bytes 524288 | tf_op jit(solution)/shard_map/all_to_all | solution.py:122
  161.2 0.7 copy-start.12
  165.1 1.4 copy-start.13
  166.4 0.8 copy-start.2
  166.4 1.6 copy-start.10
  166.4 1.6 copy-start.14
  679.3 101.9 %copy-start.11 = (f32[16]{0:T(128)}, f32[16]{0:T(128)S(1)}, u32[]{:S(2)}) copy-start(f32[16]{0:T(128)S(1)} %get-tuple-element.71) | copy-start | bytes 196
where the time goes:
time: 784 us; the launch traced here: 782 us
  blocking collectives  738 us (94%)
  other arithmetic  12.5 us (2%)
  starting transfers between devices  10.4 us (1%)
  local copies, waits for them, and re-layouts  10.2 us (1%)
    unnamed x3, blocking collectives  301 us
    psum x2, blocking collectives, squares(): return lax.psum(jnp.sum(current * current), ('row', 'space'))  199 us
    all_gather x1, blocking collectives, shards(): everyone = lax.all_gather(placed, ('row', 'space'), axis=1, tiled=True)  138 us
    psum x1, blocking collectives, shards(): alpha = norm_now / lax.psum(jnp.sum(direction * image), ('row', 'space'))  99.4 us
  transfers between devices with their start and end apart: 1, of which 0 were waited for; matrix products, arithmetic and copies ran while one was open for 1% of the time, Pallas kernels for 0%

commit v1 on v0

--- a/solution.py
+++ b/solution.py
@@ -138,7 +138,8 @@
     diag = lookup(species, hardness) + inverse_root_pi / sigma
     placed = jnp.concatenate([positions, sigma[None, :]], axis=0)
     own_labels = (row_at * lanes + space_at) * atoms + jnp.arange(atoms, dtype=jnp.int32)
-    everyone = lax.all_gather(placed, ("row", "space"), axis=1, tiled=True)
+    repeated = jnp.stack([placed] * lax.axis_size(("row", "space")))
+    everyone = jnp.concatenate(lax.all_to_all(repeated, ("row", "space"), 0, 0), axis=1)
     all_labels = jnp.arange(everyone.shape[1], dtype=jnp.int32)
 
     def spread_out(vector):

time: 784 us -> 680 us (0.87)
  blocking collectives: 738 us -> 612 us
  starting transfers between devices: 10.4 us -> 28.9 us
    all_gather x1 -> x0, blocking collectives: 138 us -> none  [shards(): everyone = lax.all_gather(placed, ('row', 'space'), axis=1, tiled=True)]
    all_to_all x0 -> x1, starting transfers between devices: none -> 18.5 us  [shards(): lax.all_to_all(repeated, ('row', 'space'), 0, 0)]
    unnamed x3, blocking collectives: 301 us -> 312 us
  transfers between devices with their start and end apart: 1 -> 2, of which waited for: 0 -> 1; matrix products, arithmetic and copies ran while one was open for 1% -> 2% of each run, Pallas kernels for 0% -> 0%
where the time goes in v1:
time: 680 us; the launch traced here: 679 us
  blocking collectives  612 us (90%)
  starting transfers between devices  28.9 us (4%)
  other arithmetic  13.2 us (2%)
  local copies, waits for them, and re-layouts  11.4 us (2%)
    unnamed x3, blocking collectives  312 us
    psum x2, blocking collectives, squares(): return lax.psum(jnp.sum(current * current), ('row', 'space'))  200 us
    psum x1, blocking collectives, shards(): alpha = norm_now / lax.psum(jnp.sum(direction * image), ('row', 'space'))  99.7 us
    all_to_all x1, starting transfers between devices, shards(): lax.all_to_all(repeated, ('row', 'space'), 0, 0)  18.5 us
  transfers between devices with their start and end apart: 2, of which 1 were waited for; matrix products, arithmetic and copies ran while one was open for 2% of the time, Pallas kernels for 0%

profile of v1, /device:TPU:1, one launch (start us, length us, event | category | flops | bytes accessed | tf_op | source)
XLA Modules:
  0.0 678.8 jit_solution(423173605246122401)
XLA Ops:
  0.6 0.8 reshape_squeeze.6
  1.5 0.7 compare_and_fusion
  2.3 3.6 gather_fusion
  5.9 0.9 broadcast_select_fusion
  6.8 10.4 %all-to-all-start = ((bf16[32,32,128]{2,1,0:T(8,128)(2,1)}), bf16[32,32,128]{2,1,0:T(8,128)(2,1)S(1)}, u32[]{:S(2)}, u32[]{:S(2)}) async-start(bf16[32,32,128]{2,1,0:T(8,128)(2,1)} %broadcast_select_fusion), calls=%async_computation | async-start | bytes 524288 | tf_op jit(solution)/shard_map/all_to_all | solution.py:122
  17.4 0.7 fusion.43
  18.0 0.7 fusion.44
  18.7 0.7 fusion.45
  19.5 2.5 fusion.40
  22.7 0.7 multiply_convert_fusion.3
  23.4 2.8 all-to-all-done
  26.3 1.1 stack.20
  27.4 18.5 %all-to-all-start.1 = ((f32[512,4,16]{2,1,0:T(4,128)}), f32[512,4,16]{2,1,0:T(4,128)S(1)}, u32[]{:S(2)}, u32[]{:S(2)}) async-start(f32[512,4,16]{2,1,0:T(4,128)} %stack.20), calls=%async_computation.1 | async-start | bytes 2097152 | tf_op jit(solution)/shard_map/all_to_all | solution.py:142
  46.2 2.0 gather_fusion.1
  49.5 0.7 add_convert_fusion
  50.2 2.7 fusion.1
  53.2 111.5 %all-reduce = f32[8192]{0:T(1024)S(1)} all-reduce(f32[8192]{0:T(1024)S(1)} %dynamic-update-slice), channel_id=1, replica_groups=mesh['row'=16,'space'=32] {'row','space'}, use_global_device_ids=true, to_apply=%add | all-reduce | flops 8192 | bytes 65536
  164.7 0.9 fusion.19
  165.8 0.4 sub.75
  166.5 0.5 multiply_reduce_fusion.8
  166.9 3.1 multiply_reduce_fusion.12
  170.1 100.5 %all-reduce.3 = (f32[]{:T(128)}, f32[]{:T(128)}) all-reduce(f32[]{:T(128)} %get-tuple-element.67, f32[]{:T(128)} %get-tuple-element.66), channel_id=1, replica_groups=mesh['row'=16,'space'=32] {'row','space'}, use_global_device_ids=true, to_apply=%region_3.4 | all-reduce | flops 2 | bytes 16 | tf_op jit(solution)/shard_map/psum | solution.py:153
  271.9 0.6 multiply_reduce_fusion.11
  272.5 99.7 %psum.30 = f32[]{:T(128)} all-reduce(f32[]{:T(128)} %get-tuple-element.83), channel_id=1, replica_groups=mesh['row'=16,'space'=32] {'row','space'}, use_global_device_ids=true, to_apply=%region_9.10 | all-reduce | flops 1 | bytes 8 | tf_op jit(solution)/shard_map/psum | solution.py:153
  373.7 100.2 %all-reduce.1 = f32[8192]{0:T(1024)S(1)} all-reduce(f32[8192]{0:T(1024)S(1)} %get-tuple-element.81), channel_id=1, replica_groups=mesh['row'=16,'space'=32] {'row','space'}, use_global_device_ids=true, to_apply=%add.1 | all-reduce | flops 8192 | bytes 65536
  474.2 0.6 multiply_reduce_fusion.10
  474.8 99.7 %psum.31 = f32[]{:T(128)} all-reduce(f32[]{:T(128)} %multiply_reduce_fusion.10), channel_id=1, replica_groups=mesh['row'=16,'space'=32] {'row','space'}, use_global_device_ids=true, to_apply=%region_12.13 | all-reduce | flops 1 | bytes 8 | tf_op jit(solution)/shard_map/psum | solution.py:161
  576.2 100.0 %all-reduce.2 = f32[8192]{0:T(1024)S(1)} all-reduce(f32[8192]{0:T(1024)S(1)} %dynamic-update-slice.2), channel_id=1, replica_groups=mesh['row'=16,'space'=32] {'row','space'}, use_global_device_ids=true, to_apply=%add.2 | all-reduce | flops 8192 | bytes 65536
  676.2 0.9 multiply_reduce_fusion.2
  677.2 0.4 multiply_reduce_fusion
  677.6 0.6 pad_maximum_fusion.2
  678.2 0.6 broadcast_multiply_fusion
  (71 shorter events, 3.3 us)
Async XLA Ops:
  0.6 18.7 %copy-start = (bf16[128,256]{1,0:T(8,128)(2,1)S(1)}, bf16[128,256]{1,0:T(8,128)(2,1)}, u32[]{:S(2)}) copy-start(bf16[128,256]{1,0:T(8,128)(2,1)} %param.23) | copy-start | bytes 196612
  2.2 15.0 %copy-start.6 = (s32[512]{0:T(512)S(1)}, s32[512]{0:T(512)}, u32[]{:S(2)}) copy-start(s32[512]{0:T(512)} %param.21) | copy-start | bytes 6148
  2.2 15.1 %copy-start.4 = (f32[3,512]{1,0:T(4,128)S(1)}, f32[3,512]{1,0:T(4,128)}, u32[]{:S(2)}) copy-start(f32[3,512]{1,0:T(4,128)} %param.22) | copy-start | bytes 18436
  2.2 15.1 %copy-start.7 = (f32[4]{0:T(128)S(1)}, f32[4]{0:T(128)}, u32[]{:S(2)}) copy-start(f32[4]{0:T(128)} %param.28) | copy-start | bytes 52
  2.3 15.7 %copy-start.8 = (f32[4]{0:T(128)S(1)}, f32[4]{0:T(128)}, u32[]{:S(2)}) copy-start(f32[4]{0:T(128)} %param.29) | copy-start | bytes 52
  2.3 16.4 %copy-start.9 = (f32[4]{0:T(128)S(1)}, f32[4]{0:T(128)}, u32[]{:S(2)}) copy-start(f32[4]{0:T(128)} %param.30) | copy-start | bytes 52
  2.3 17.1 %copy-start.1 = (bf16[16,128]{1,0:T(8,128)(2,1)S(1)}, bf16[16,128]{1,0:T(8,128)(2,1)}, u32[]{:S(2)}) copy-start(bf16[16,128]{1,0:T(8,128)(2,1)} %param.16) | copy-start | bytes 12292
  2.3 17.2 %copy-start.10 = (s32[16]{0:T(128)S(1)}, s32[16]{0:T(128)}, u32[]{:S(2)}) copy-start(s32[16]{0:T(128)} %param.18) | copy-start | bytes 196
  2.3 19.7 %copy-start.5 = (f32[3,16]{1,0:T(4,128)S(1)}, f32[3,16]{1,0:T(4,128)}, u32[]{:S(2)}) copy-start(f32[3,16]{1,0:T(4,128)} %param.17) | copy-start | bytes 580
  2.3 20.4 %copy-start.12 = (f32[8,128]{1,0:T(8,128)S(1)}, f32[8,128]{1,0:T(8,128)}, u32[]{:S(2)}) copy-start(f32[8,128]{1,0:T(8,128)} %param.24) | copy-start | bytes 12292
  6.8 19.4 %all-to-all-start = ((bf16[32,32,128]{2,1,0:T(8,128)(2,1)}), bf16[32,32,128]{2,1,0:T(8,128)(2,1)S(1)}, u32[]{:S(2)}, u32[]{:S(2)}) async-start(bf16[32,32,128]{2,1,0:T(8,128)(2,1)} %broadcast_select_fusion), calls=%async_computation | async-start | bytes 524288 | tf_op jit(solution)/shard_map/all_to_all | solution.py:122
  27.4 137.3 %all-to-all-start.1 = ((f32[512,4,16]{2,1,0:T(4,128)}), f32[512,4,16]{2,1,0:T(4,128)S(1)}, u32[]{:S(2)}, u32[]{:S(2)}) async-start(f32[512,4,16]{2,1,0:T(4,128)} %stack.20), calls=%async_computation.1 | async-start | bytes 2097152 | tf_op jit(solution)/shard_map/all_to_all | solution.py:142
  46.2 2.1 copy-start.2
  48.2 0.7 copy-start.13
  48.6 0.8 copy-start.3
  48.6 1.6 copy-start.14
  575.9 101.7 %copy-start.11 = (f32[16]{0:T(128)}, f32[16]{0:T(128)S(1)}, u32[]{:S(2)}) copy-start(f32[16]{0:T(128)S(1)} %get-tuple-element.71) | copy-start | bytes 196
